TPU v7x, 32 devices: a whole 2x2x4 slice. The times are simulated.
32 devices in a mesh: row: 8 (over z, x), pair: 4 (over y, core).
Axes of the slice: x: 2, y: 2, z: 4, core: 2. Of those that a mesh axis runs over, the one named last changes fastest.
Arguments:
- matrix: float32 [1536, 2048], P('row', 'pair'), may hold values from -50 to 50
- seating: int32 [8], replicated, may hold values from 0 to 7, each once
Outputs:
- rotated: float32 [1536, 2048], P('row', 'pair')
All inputs are finite; a program needn't handle non-finite values.
Results may differ from a plain program's by a relative error of at most 0.0003.
Values sent between devices are 32-bit elements; how exact they have to be, the bound alone decides.
A program may use at most 64 MiB of HBM per device.

v0:
```python
import jax
import jax.numpy as jnp
from jax import lax
from jax.sharding import PartitionSpec as P

B = 256
STEPS = 4
INNER = 4


def shifted(block, axis, distance):
    devices = range(lax.axis_size(axis))
    route = [(i - distance, i) for i in devices if i - distance in devices]
    return lax.ppermute(block, axis, route)


def columns_turn(block, cosines, sines):
    left = block[:, :B]
    right = block[:, B:]
    return jnp.concatenate([cosines * left - sines * right, sines * left + cosines * right], axis=1)


def rows_turn(block, cosines, sines):
    left = block[:B]
    right = block[B:]
    return jnp.concatenate(
        [
            cosines[:, None] * left - sines[:, None] * right,
            sines[:, None] * left + cosines[:, None] * right,
        ],
        axis=0,
    )


def roll_lower(block, axis_number):
    if axis_number == 1:
        return jnp.concatenate([block[:, :B], jnp.roll(block[:, B:], -1, axis=1)], axis=1)
    return jnp.concatenate([block[:B], jnp.roll(block[B:], -1, axis=0)], axis=0)


def solve_pair(gram):
    rotation = jnp.eye(2 * B, dtype=jnp.float32)
    for sweep in range(INNER):
        whole_diag = jnp.diagonal(gram)
        upper_diag = whole_diag[:B]
        lower_diag = whole_diag[B:]
        coupling = jnp.diagonal(gram[:B, B:])
        differ = lower_diag - upper_diag
        signs = jnp.where(differ >= 0.0, 1.0, -1.0).astype(jnp.float32)
        denom = jnp.abs(differ) + jnp.sqrt(
            differ * differ + 4.0 * coupling * coupling + 1e-12 * (upper_diag + lower_diag) ** 2
        )
        tangent = 2.0 * signs * coupling / denom
        cosines = 1.0 / jnp.sqrt(1.0 + tangent * tangent)
        sines = tangent * cosines
        gram = rows_turn(columns_turn(gram, cosines, sines), cosines, sines)
        rotation = columns_turn(rotation, cosines, sines)
        gram = roll_lower(roll_lower(gram, 1), 0)
        rotation = roll_lower(rotation, 1)
    rotation = jnp.concatenate([rotation[:, :B], jnp.roll(rotation[:, B:], INNER, axis=1)], axis=1)
    return (rotation, gram)


def product(left, right):
    return jnp.dot(left, right, precision=lax.Precision.HIGHEST, preferred_element_type=jnp.float32)


def local(matrix, seating):
    height = matrix.shape[0]
    place = lax.axis_index("pair")
    tables = lax.axis_size("pair")
    wanted = lax.dynamic_slice(seating, (2 * place,), (2,))
    piece = lax.all_gather(matrix, "pair", axis=1, tiled=True)
    count = piece.shape[1] // B
    shaped = piece.reshape(height, count, B)
    labels = jnp.arange(count, dtype=jnp.int32)
    upper_part = jnp.sum(jnp.where((labels == wanted[0])[None, :, None], shaped, 0.0), axis=1)
    lower_part = jnp.sum(jnp.where((labels == wanted[1])[None, :, None], shaped, 0.0), axis=1)
    upper = upper_part
    lower = lower_part
    first_table = place == 0
    last_table = place == tables - 1
    for step in range(STEPS):
        joined = jnp.concatenate([upper, lower], axis=1)
        gram = lax.psum(product(joined.T, joined), "row")
        rotation, turned = solve_pair(gram)
        result = product(joined, rotation)
        upper = result[:, :B]
        lower = result[:, B:]
        sent_up = jnp.where(first_table, lower, upper)
        arrived_up = shifted(sent_up, "pair", 1)
        arrived_down = shifted(lower, "pair", -1)
        new_upper = jnp.where(first_table, upper, arrived_up)
        new_lower = jnp.where(last_table, upper, arrived_down)
        upper, lower = (new_upper, new_lower)
    return jnp.concatenate([upper, lower], axis=1)


def solution(mesh):
    in_specs = (P("row", "pair"), P())
    out_specs = P("row", "pair")
    return jax.shard_map(local, mesh=mesh, in_specs=in_specs, out_specs=out_specs, check_vma=False)
```

profile of v0, /device:TPU:1, one launch (start us, length us, event | category | flops | bytes accessed | tf_op | source)
XLA Modules:
  0.0 589.1 jit_solution(15412521582223082813)
XLA Ops:
  10.0 21.1 %all-gather.2.cloned.1.call-done = f32[192,2048]{1,0:T(8,128)} async-done(((f32[192,512]{1,0:T(8,128)}), f32[192,2048]{1,0:T(8,128)}) %all-gather.2.cloned.1.call-update) | async-done | bytes 1572880 | tf_op jit(solution)/shard_map/all_gather | solution.py:73
  37.0 76.5 %all-reduce.5.cloned.1.call-done = f32[512,512]{1,0:T(8,128)} async-done(((f32[512,512]{1,0:T(8,128)}), f32[512,512]{1,0:T(8,128)}) %all-reduce.5.cloned.1.call-update) | async-done | bytes 1048592 | tf_op jit(solution)/shard_map/psum | solution.py:85
  114.5 2.3 gather_fusion.1
  116.9 4.5 gather_fusion
  124.4 4.5 gather_fusion.2
  129.0 2.3 gather_fusion.3
  140.1 4.5 gather_fusion.4
  149.6 4.5 gather_fusion.6
  160.3 4.3 collective-permute-start
  167.3 4.4 collective-permute-done.1
  174.8 75.4 %all-reduce.7.cloned.1.call-done = f32[512,512]{1,0:T(8,128)} async-done(((f32[512,512]{1,0:T(8,128)}), f32[512,512]{1,0:T(8,128)}) %all-reduce.7.cloned.1.call-update) | async-done | bytes 1048592 | tf_op jit(solution)/shard_map/psum | solution.py:85
  253.6 4.5 gather_fusion.8
  261.1 4.5 gather_fusion.10
  265.7 2.3 gather_fusion.11
  276.8 4.5 gather_fusion.12
  286.3 4.5 gather_fusion.14
  297.0 4.3 collective-permute-start.2
  304.0 4.4 collective-permute-done.3
  311.6 75.3 %all-reduce.9.cloned.1.call-done = f32[512,512]{1,0:T(8,128)} async-done(((f32[512,512]{1,0:T(8,128)}), f32[512,512]{1,0:T(8,128)}) %all-reduce.9.cloned.1.call-update) | async-done | bytes 1048592 | tf_op jit(solution)/shard_map/psum | solution.py:85
  390.3 4.5 gather_fusion.16
  397.8 4.5 gather_fusion.18
  413.5 4.5 gather_fusion.20
  423.0 4.5 gather_fusion.22
  433.7 4.3 collective-permute-start.4
  440.7 4.4 collective-permute-done.5
  448.0 75.8 %all-reduce.11.cloned.1.call-done = f32[512,512]{1,0:T(8,128)} async-done(((f32[512,512]{1,0:T(8,128)}), f32[512,512]{1,0:T(8,128)}) %all-reduce.11.cloned.1.call-update) | async-done | bytes 1048592 | tf_op jit(solution)/shard_map/psum | solution.py:85
  527.2 4.5 gather_fusion.24
  534.7 4.5 gather_fusion.26
  550.4 4.5 gather_fusion.28
  560.6 4.5 gather_fusion.30
  570.1 4.3 collective-permute-start.6
  577.0 4.4 collective-permute-done.7
  (360 shorter events, 135.5 us)
Async XLA Ops:
  6.5 24.6 %all-gather.2.cloned.1.call-start = ((), (), s32[]{:S(2)}) async-start(), calls=%async_computation | async-start | bytes 1966080 | tf_op jit(solution)/shard_map/all_gather | solution.py:73
  7.3 106.2 %all-reduce.5.cloned.1.call-start = ((), (), s32[]{:S(2)}) async-start(), calls=%async_computation.1 | async-start | bytes 2097152 | tf_op jit(solution)/shard_map/psum | solution.py:85
  36.2 213.9 %all-reduce.7.cloned.1.call-start = ((), (), s32[]{:S(2)}) async-start(), calls=%async_computation.2 | async-start | bytes 2097152 | tf_op jit(solution)/shard_map/psum | solution.py:85
  124.3 7.0 %copy-start.28 = (f32[512,1]{1,0:T(8,128)}, f32[512,1]{1,0:T(8,128)S(1)}, u32[]{:S(2)}) copy-start(f32[512,1]{1,0:T(8,128)S(1)} %slice.1122) | copy-start | bytes 6148
  140.1 4.6 copy-start.5
  140.1 4.6 copy-start.24
  149.6 6.9 %copy-start.6 = (f32[512,255]{1,0:T(8,128)S(1)}, f32[512,255]{1,0:T(8,128)}, u32[]{:S(2)}) copy-start(f32[512,255]{1,0:T(8,128)} %slice.1123) | copy-start | bytes 1566724
  160.3 6.9 %collective-permute-start = (f32[192,256]{1,0:T(8,128)S(1)}, f32[192,256]{1,0:T(8,128)S(1)}, u32[]{:S(2)}, u32[]{:S(2)}) collective-permute-start(f32[192,256]{1,0:T(8,128)S(1)} %get-tuple-element.117), channel_id=1, source_target_pairs={{0,1},{1,2},{2,3},{4,5},{5,6},{6,7},{8,9},{9,10},{10,11},{12,13},{... | collective-permute-start | bytes 589832 | tf_op jit(solution)/shard_map/ppermute | solution.py:14
  164.7 7.0 %collective-permute-start.1 = (f32[192,256]{1,0:T(8,128)S(1)}, f32[192,256]{1,0:T(8,128)S(1)}, u32[]{:S(2)}, u32[]{:S(2)}) collective-permute-start(f32[192,256]{1,0:T(8,128)S(1)} %get-tuple-element.118), channel_id=1, source_target_pairs={{1,0},{2,1},{3,2},{5,4},{6,5},{7,6},{9,8},{10,9},{11,10},{13,12},{... | collective-permute-start | bytes 589832 | tf_op jit(solution)/shard_map/ppermute | solution.py:14
  174.6 212.3 %all-reduce.9.cloned.1.call-start = ((), (), s32[]{:S(2)}) async-start(), calls=%async_computation.3 | async-start | bytes 2097152 | tf_op jit(solution)/shard_map/psum | solution.py:85
  261.0 7.0 %copy-start.29 = (f32[512,1]{1,0:T(8,128)}, f32[512,1]{1,0:T(8,128)S(1)}, u32[]{:S(2)}) copy-start(f32[512,1]{1,0:T(8,128)S(1)} %slice.1164) | copy-start | bytes 6148
  276.8 4.6 copy-start.7
  276.8 4.6 copy-start.25
  286.3 6.9 %copy-start.8 = (f32[512,255]{1,0:T(8,128)S(1)}, f32[512,255]{1,0:T(8,128)}, u32[]{:S(2)}) copy-start(f32[512,255]{1,0:T(8,128)} %slice.1165) | copy-start | bytes 1566724
  297.0 6.9 %collective-permute-start.2 = (f32[192,256]{1,0:T(8,128)S(1)}, f32[192,256]{1,0:T(8,128)S(1)}, u32[]{:S(2)}, u32[]{:S(2)}) collective-permute-start(f32[192,256]{1,0:T(8,128)S(1)} %get-tuple-element.113), channel_id=1, source_target_pairs={{0,1},{1,2},{2,3},{4,5},{5,6},{6,7},{8,9},{9,10},{10,11},{12,13},{... | collective-permute-start | bytes 589832 | tf_op jit(solution)/shard_map/ppermute | solution.py:14
  301.4 7.0 %collective-permute-start.3 = (f32[192,256]{1,0:T(8,128)S(1)}, f32[192,256]{1,0:T(8,128)S(1)}, u32[]{:S(2)}, u32[]{:S(2)}) collective-permute-start(f32[192,256]{1,0:T(8,128)S(1)} %get-tuple-element.114), channel_id=1, source_target_pairs={{1,0},{2,1},{3,2},{5,4},{6,5},{7,6},{9,8},{10,9},{11,10},{13,12},{... | collective-permute-start | bytes 589832 | tf_op jit(solution)/shard_map/ppermute | solution.py:14
  311.3 212.4 %all-reduce.11.cloned.1.call-start = ((), (), s32[]{:S(2)}) async-start(), calls=%async_computation.4 | async-start | bytes 2097152 | tf_op jit(solution)/shard_map/psum | solution.py:85
  386.9 3.4 copy-start.2
  397.7 7.0 %copy-start.30 = (f32[512,1]{1,0:T(8,128)}, f32[512,1]{1,0:T(8,128)S(1)}, u32[]{:S(2)}) copy-start(f32[512,1]{1,0:T(8,128)S(1)} %slice.1206) | copy-start | bytes 6148
  413.5 4.6 copy-start.9
  413.5 4.6 copy-start.26
  423.0 6.9 %copy-start.10 = (f32[512,255]{1,0:T(8,128)S(1)}, f32[512,255]{1,0:T(8,128)}, u32[]{:S(2)}) copy-start(f32[512,255]{1,0:T(8,128)} %slice.1207) | copy-start | bytes 1566724
  433.7 6.9 %collective-permute-start.4 = (f32[192,256]{1,0:T(8,128)S(1)}, f32[192,256]{1,0:T(8,128)S(1)}, u32[]{:S(2)}, u32[]{:S(2)}) collective-permute-start(f32[192,256]{1,0:T(8,128)S(1)} %get-tuple-element.109), channel_id=1, source_target_pairs={{0,1},{1,2},{2,3},{4,5},{5,6},{6,7},{8,9},{9,10},{10,11},{12,13},{... | collective-permute-start | bytes 589832 | tf_op jit(solution)/shard_map/ppermute | solution.py:14
  438.1 7.0 %collective-permute-start.5 = (f32[192,256]{1,0:T(8,128)S(1)}, f32[192,256]{1,0:T(8,128)S(1)}, u32[]{:S(2)}, u32[]{:S(2)}) collective-permute-start(f32[192,256]{1,0:T(8,128)S(1)} %get-tuple-element.110), channel_id=1, source_target_pairs={{1,0},{2,1},{3,2},{5,4},{6,5},{7,6},{9,8},{10,9},{11,10},{13,12},{... | collective-permute-start | bytes 589832 | tf_op jit(solution)/shard_map/ppermute | solution.py:14
  534.6 7.0 %copy-start.27 = (f32[512,1]{1,0:T(8,128)}, f32[512,1]{1,0:T(8,128)S(1)}, u32[]{:S(2)}) copy-start(f32[512,1]{1,0:T(8,128)S(1)} %slice.1248) | copy-start | bytes 6148
  550.4 4.6 copy-start.4
  550.4 4.6 copy-start.23
  560.6 6.9 %copy-start.31 = (f32[512,256]{1,0:T(8,128)S(1)}, f32[512,256]{1,0:T(8,128)}, u32[]{:S(2)}) copy-start(f32[512,256]{1,0:T(8,128)} %get-tuple-element.120) | copy-start | bytes 1572868
  560.6 6.9 %copy-start.32 = (f32[512,255]{1,0:T(8,128)S(1)}, f32[512,255]{1,0:T(8,128)}, u32[]{:S(2)}) copy-start(f32[512,255]{1,0:T(8,128)} %slice.1251) | copy-start | bytes 1566724
  560.6 7.0 %copy-start.33 = (f32[512,1]{1,0:T(8,128)S(1)}, f32[512,1]{1,0:T(8,128)}, u32[]{:S(2)}) copy-start(f32[512,1]{1,0:T(8,128)} %slice.1252) | copy-start | bytes 6148
  570.1 6.9 %collective-permute-start.6 = (f32[192,256]{1,0:T(8,128)S(1)}, f32[192,256]{1,0:T(8,128)S(1)}, u32[]{:S(2)}, u32[]{:S(2)}) collective-permute-start(f32[192,256]{1,0:T(8,128)S(1)} %get-tuple-element.105), channel_id=1, source_target_pairs={{0,1},{1,2},{2,3},{4,5},{5,6},{6,7},{8,9},{9,10},{10,11},{12,13},{... | collective-permute-start | bytes 589832 | tf_op jit(solution)/shard_map/ppermute | solution.py:14
  574.5 7.0 %collective-permute-start.7 = (f32[192,256]{1,0:T(8,128)S(1)}, f32[192,256]{1,0:T(8,128)S(1)}, u32[]{:S(2)}, u32[]{:S(2)}) collective-permute-start(f32[192,256]{1,0:T(8,128)S(1)} %get-tuple-element.106), channel_id=1, source_target_pairs={{1,0},{2,1},{3,2},{5,4},{6,5},{7,6},{9,8},{10,9},{11,10},{13,12},{... | collective-permute-start | bytes 589832 | tf_op jit(solution)/shard_map/ppermute | solution.py:14
  (39 other events, 47.9 us)
Sparse Core Ops, SparseCore 0:
  8.9 22.1 all-gather.1
  36.4 77.0 all-reduce.4
  174.7 75.4 all-reduce.6
  311.4 75.4 all-reduce.8
  448.1 75.5 all-reduce.10
where the time goes:
time: 593 us; the launch traced here: 589 us
  waiting for transfers between devices  345 us (58%)
  local copies, waits for them, and re-layouts  155 us (26%)
  other arithmetic  34.3 us (6%)
  starting transfers between devices  26.4 us (4%)
  between operations  15.2 us (3%)
  matrix products  13 us (2%)
    psum x4, waiting for transfers between devices, local(): gram = lax.psum(product(joined.T, joined), 'row')  303 us
    gather x16, local copies, waits for them, and re-layouts, solve_pair(): whole_diag = jnp.diagonal(gram)  72.3 us
    gather x16, local copies, waits for them, and re-layouts, solve_pair(): coupling = jnp.diagonal(gram[:B, B:])  37.5 us
    ppermute x8, starting transfers between devices, shifted(): return lax.ppermute(block, axis, route)  25.3 us
    all_gather x1, waiting for transfers between devices, local(): piece = lax.all_gather(matrix, 'pair', axis=1, tiled=True)  21.1 us
    ppermute x8, waiting for transfers between devices, shifted(): return lax.ppermute(block, axis, route)  20 us
    sub x16, other arithmetic, columns_turn(): cosines * left - sines * right  15.2 us
    unnamed x101, local copies, waits for them, and re-layouts  15.2 us
  transfers between devices with their start and end apart: 13, of which 13 were waited for; matrix products, arithmetic and copies ran while one was open for 0% of the time, Pallas kernels for 0%

commit v1 on v0

v1 whole, which is shorter than its diff:
```python
import jax
import jax.numpy as jnp
from jax import lax
from jax.sharding import PartitionSpec as P

B = 256
STEPS = 4
INNER = 4


def shifted(block, axis, distance):
    devices = range(lax.axis_size(axis))
    route = [(i - distance, i) for i in devices if i - distance in devices]
    return lax.ppermute(block, axis, route)


def ahead(values, distance):
    return jnp.roll(values, -distance, axis=-1) if distance else values


def band_sums(upper, lower):
    rows = []
    for o in range(INNER):
        u, l = ahead(upper, o), ahead(lower, o)
        rows += [upper * u, lower * l, upper * l]
        if o:
            rows += [lower * u]
    return jnp.stack([jnp.sum(row, axis=0) for row in rows])


def solve_bands(bands):
    uu, ll, ul, lu = {}, {}, {}, {}
    at = 0
    for o in range(INNER):
        uu[o], ll[o], ul[o] = bands[at], bands[at + 1], bands[at + 2]
        at += 3
        if o:
            lu[o] = bands[at]
            at += 1
    turns = []
    for sweep in range(INNER):
        differ = ll[0] - uu[0]
        coupling = ul[0]
        signs = jnp.where(differ >= 0.0, 1.0, -1.0).astype(jnp.float32)
        total = uu[0] + ll[0]
        denom = jnp.abs(differ) + jnp.sqrt(
            differ * differ + 4.0 * coupling * coupling + 1e-12 * (total * total)
        )
        tangent = 2.0 * signs * coupling / denom
        c = 1.0 / jnp.sqrt(1.0 + tangent * tangent)
        s = tangent * c
        turns.append((c, s))
        reach = INNER - 1 - sweep
        if reach == 0:
            break
        new_uu, new_ll, new_ul, new_lu = {}, {}, {}, {}
        for o in range(reach + 1):
            cj, sj = ahead(c, o), ahead(s, o)
            a, b, d = uu[o], ul[o], ll[o]
            e = lu[o] if o else ul[0]
            top_u, top_l = c * a - s * e, c * b - s * d
            low_u, low_l = s * a + c * e, s * b + c * d
            new_ul[o] = sj * top_u + cj * top_l
            if o < reach:
                new_uu[o] = cj * top_u - sj * top_l
                new_ll[o] = sj * low_u + cj * low_l
                if o:
                    new_lu[o] = cj * low_u - sj * low_l
        uu = new_uu
        ll = {o: ahead(new_ll[o], 1) for o in new_ll}
        ul = {o: new_ul[o + 1] for o in range(reach)}
        lu = {o: ahead(new_lu[o - 1] if o > 1 else new_ul[0], 1) for o in range(1, reach)}
    return turns


def turn(upper, lower, turns):
    for k, (c, s) in enumerate(turns):
        upper, lower = c * upper - s * lower, s * upper + c * lower
        if k < INNER - 1:
            lower = ahead(lower, 1)
    return upper, ahead(lower, 1 - INNER)


def local(matrix, seating):
    height = matrix.shape[0]
    place = lax.axis_index("pair")
    tables = lax.axis_size("pair")
    wanted = lax.dynamic_slice(seating, (2 * place,), (2,))
    piece = lax.all_gather(matrix, "pair", axis=1, tiled=True)
    count = piece.shape[1] // B
    shaped = piece.reshape(height, count, B)
    labels = jnp.arange(count, dtype=jnp.int32)
    upper = jnp.sum(jnp.where((labels == wanted[0])[None, :, None], shaped, 0.0), axis=1)
    lower = jnp.sum(jnp.where((labels == wanted[1])[None, :, None], shaped, 0.0), axis=1)
    first_table = place == 0
    last_table = place == tables - 1
    for step in range(STEPS):
        bands = lax.psum(band_sums(upper, lower), "row")
        upper, lower = turn(upper, lower, solve_bands(bands))
        sent_up = jnp.where(first_table, lower, upper)
        arrived_up = shifted(sent_up, "pair", 1)
        arrived_down = shifted(lower, "pair", -1)
        new_upper = jnp.where(first_table, upper, arrived_up)
        new_lower = jnp.where(last_table, upper, arrived_down)
        upper, lower = (new_upper, new_lower)
    return jnp.concatenate([upper, lower], axis=1)


def solution(mesh):
    in_specs = (P("row", "pair"), P())
    out_specs = P("row", "pair")
    return jax.shard_map(local, mesh=mesh, in_specs=in_specs, out_specs=out_specs, check_vma=False)
```

time: 593 us -> 354 us (0.60)
  waiting for transfers between devices: 345 us -> 42.2 us
  blocking collectives: 0 us -> 109 us
  local copies, waits for them, and re-layouts: 155 us -> 46.4 us
  other arithmetic: 34.3 us -> 98.1 us
  starting transfers between devices: 26.4 us -> 42.5 us
  matrix products: 13 us -> 0 us
    psum x4 -> x0, waiting for transfers between devices: 303 us -> none  [local(): gram = lax.psum(product(joined.T, joined), 'row')]
    gather x32 -> x0, local copies, waits for them, and re-layouts: 110 us -> none  [the longest x16 72.3 us: solve_pair(): whole_diag = jnp.diagonal(gram)]
    psum x0 -> x4, blocking collectives: none -> 109 us  [local(): bands = lax.psum(band_sums(upper, lower), 'row')]
    sqrt x16 -> x8, other arithmetic: 0.29 us -> 28 us  [solve_bands(): c = 1.0 / jnp.sqrt(1.0 + tangent * tangent)]
    mul x16 -> x12, other arithmetic: 0.11 us -> 23.3 us  [solve_bands(): s = tangent * c]
    add x0 -> x40, other arithmetic: none -> 22.8 us  [the longest x16 13 us: solve_bands(): new_ll[o] = sj * low_u + cj * low_l]
    ppermute x8, starting transfers between devices: 25.3 us -> 42.5 us  [shifted(): return lax.ppermute(block, axis, route)]
    slice x72 -> x224, local copies, waits for them, and re-layouts: 29 us -> 42.8 us  [the longest x220 42.8 us: ahead(): return jnp.roll(values, -distance, axis=-1) if distance else values]
  transfers between devices with their start and end apart: 13 -> 9, of which waited for: 13 -> 9; matrix products, arithmetic and copies ran while one was open for 0% -> 1% of each run, Pallas kernels for 0% -> 0%
where the time goes in v1:
time: 354 us; the launch traced here: 352 us
  blocking collectives  109 us (31%)
  other arithmetic  98.1 us (28%)
  local copies, waits for them, and re-layouts  46.4 us (13%)
  starting transfers between devices  42.5 us (12%)
  waiting for transfers between devices  42.2 us (12%)
  between operations  14.5 us (4%)
    psum x4, blocking collectives, local(): bands = lax.psum(band_sums(upper, lower), 'row')  109 us
    slice x220, local copies, waits for them, and re-layouts, ahead(): return jnp.roll(values, -distance, axis=-1) if distance else values  42.8 us
    ppermute x8, starting transfers between devices, shifted(): return lax.ppermute(block, axis, route)  42.5 us
    sqrt x8, other arithmetic, solve_bands(): c = 1.0 / jnp.sqrt(1.0 + tangent * tangent)  28 us
    mul x12, other arithmetic, solve_bands(): s = tangent * c  23.3 us
    all_gather x1, waiting for transfers between devices, local(): piece = lax.all_gather(matrix, 'pair', axis=1, tiled=True)  21.3 us
    ppermute x8, waiting for transfers between devices, shifted(): return lax.ppermute(block, axis, route)  20.2 us
    sub x8, other arithmetic, solve_bands(): top_u, top_l = (c * a - s * e, c * b - s * d)  13.1 us
  transfers between devices with their start and end apart: 9, of which 9 were waited for; matrix products, arithmetic and copies ran while one was open for 1% of the time, Pallas kernels for 0%

profile of v1, /device:TPU:1, one launch (start us, length us, event | category | flops | bytes accessed | tf_op | source)
XLA Modules:
  0.0 352.5 jit_solution(764003190726804659)
XLA Ops:
  9.8 21.3 %all-gather.2.cloned.1.call-done = f32[192,2048]{1,0:T(8,128)} async-done(((f32[192,512]{1,0:T(8,128)}), f32[192,2048]{1,0:T(8,128)}) %all-gather.2.cloned.1.call-update) | async-done | bytes 1572880 | tf_op jit(solution)/shard_map/all_gather | solution.py:89
  35.4 29.8 %psum.28 = f32[15,256]{1,0:T(8,128)S(1)} all-reduce(f32[15,256]{1,0:T(8,128)S(1)} %stack.207), channel_id=1, replica_groups=mesh['row'=8,'pair'=4] {'row'}, use_global_device_ids=true, to_apply=%region_17.18 | all-reduce | flops 3840 | bytes 30720 | tf_op jit(solution)/shard_map/psum | solution.py:98
  67.7 2.6 fusion.182
  73.5 2.0 multiply_add_fusion.63
  78.1 5.0 %fusion.218 = (f32[256]{0:T(256)S(1)}, f32[256]{0:T(256)S(1)}, f32[256]{0:T(256)S(1)}, f32[256]{0:T(256)S(1)}, f32[256]{0:T(256)S(1)}, /*index=5*/f32[256]{0:T(256)S(1)}) fusion(f32[1]{0:T(128)} %slice.972, f32[255]{0:T(256)S(1)} %slice.971, f32[1]{0:T(128)} %slice.962, f32[255]{0:T(256)S(1)} %slice.961, f32[256]{0:T(256)S(1)} %get-tuple-element.224, ...), kind=kLoop, calls=%fused_computation.759 | loop fusion | flops 18176 | bytes 28672 | tf_op jit(solution)/shard_map/mul | solution.py:51
  83.2 2.5 multiply_add_fusion.61
  91.0 7.0 %add_rsqrt_fusion.21 = (f32[1,256]{1,0:T(1,128)S(1)}, f32[1,256]{1,0:T(1,128)S(1)}, f32[1,256]{1,0:T(1,128)S(1)}) fusion(f32[1,1]{1,0:T(1,128)} %bitcast.69, f32[1,255]{1,0:T(1,128)S(1)} %bitcast.655, f32[1,1]{1,0:T(1,128)} %bitcast.67, f32[1,255]{1,0:T(1,128)S(1)} %bitcast.659, f32[15,256]{1,0:T(8,128)S(1)} %psum.28, f32[1,3]{1,0:T(1,128)S(1)} %slice_bitcast_fusion.12, ...), kind=kLoop, calls=%fused_computation.688 | loop fusion | flops 30720 | bytes 34816 | tf_op jit(solution)/shard_map/sqrt | solution.py:50
  98.7 9.6 %collective-permute-start = (f32[192,256]{1,0:T(8,128)S(1)}, f32[192,256]{1,0:T(8,128)S(1)}, u32[]{:S(2)}, u32[]{:S(2)}) collective-permute-start(f32[192,256]{1,0:T(8,128)S(1)} %get-tuple-element.210), channel_id=1, source_target_pairs={{0,1},{1,2},{2,3},{4,5},{5,6},{6,7},{8,9},{9,10},{10,11},{12,13},{... | collective-permute-start | bytes 589832 | tf_op jit(solution)/shard_map/ppermute | solution.py:14
  110.9 4.4 %collective-permute-done.1 = f32[192,256]{1,0:T(8,128)S(1)} collective-permute-done((f32[192,256]{1,0:T(8,128)S(1)}, f32[192,256]{1,0:T(8,128)S(1)}, u32[]{:S(2)}, u32[]{:S(2)}) %collective-permute-start.1) | collective-permute-done | bytes 196640 | tf_op jit(solution)/shard_map/ppermute | solution.py:14
  116.6 26.3 %psum.29 = f32[15,256]{1,0:T(8,128)S(1)} all-reduce(f32[15,256]{1,0:T(8,128)S(1)} %stack.223), channel_id=1, replica_groups=mesh['row'=8,'pair'=4] {'row'}, use_global_device_ids=true, to_apply=%region_33.34 | all-reduce | flops 3840 | bytes 30720 | tf_op jit(solution)/shard_map/psum | solution.py:98
  145.4 2.6 fusion.191
  155.9 5.0 %fusion.220 = (f32[256]{0:T(256)S(1)}, f32[256]{0:T(256)S(1)}, f32[256]{0:T(256)S(1)}, f32[256]{0:T(256)S(1)}, f32[256]{0:T(256)S(1)}, /*index=5*/f32[256]{0:T(256)S(1)}) fusion(f32[1]{0:T(128)} %slice.1049, f32[255]{0:T(256)S(1)} %slice.1048, f32[1]{0:T(128)} %slice.1039, f32[255]{0:T(256)S(1)} %slice.1038, f32[256]{0:T(256)S(1)} %get-tuple-element.199, ...), kind=kLoop, calls=%fused_computation.761 | loop fusion | flops 18176 | bytes 28672 | tf_op jit(solution)/shard_map/mul | solution.py:51
  160.9 2.5 multiply_add_fusion.46
  168.7 7.0 %add_rsqrt_fusion.14 = (f32[1,256]{1,0:T(1,128)S(1)}, f32[1,256]{1,0:T(1,128)S(1)}, f32[1,256]{1,0:T(1,128)S(1)}) fusion(f32[1,1]{1,0:T(1,128)} %bitcast.145, f32[1,255]{1,0:T(1,128)S(1)} %bitcast.656, f32[1,1]{1,0:T(1,128)} %bitcast.143, f32[1,255]{1,0:T(1,128)S(1)} %bitcast.660, f32[15,256]{1,0:T(8,128)S(1)} %psum.29, f32[1,3]{1,0:T(1,128)S(1)} %slice_bitcast_fusion.8, ...), kind=kLoop, calls=%fused_computation.643 | loop fusion | flops 30720 | bytes 34816 | tf_op jit(solution)/shard_map/sqrt | solution.py:50
  176.4 8.4 %collective-permute-start.2 = (f32[192,256]{1,0:T(8,128)S(1)}, f32[192,256]{1,0:T(8,128)S(1)}, u32[]{:S(2)}, u32[]{:S(2)}) collective-permute-start(f32[192,256]{1,0:T(8,128)S(1)} %get-tuple-element.185), channel_id=1, source_target_pairs={{0,1},{1,2},{2,3},{4,5},{5,6},{6,7},{8,9},{9,10},{10,11},{12,13},{... | collective-permute-start | bytes 589832 | tf_op jit(solution)/shard_map/ppermute | solution.py:14
  187.4 4.4 %collective-permute-done.3 = f32[192,256]{1,0:T(8,128)S(1)} collective-permute-done((f32[192,256]{1,0:T(8,128)S(1)}, f32[192,256]{1,0:T(8,128)S(1)}, u32[]{:S(2)}, u32[]{:S(2)}) %collective-permute-start.3) | collective-permute-done | bytes 196640 | tf_op jit(solution)/shard_map/ppermute | solution.py:14
  193.1 26.3 %psum.30 = f32[15,256]{1,0:T(8,128)S(1)} all-reduce(f32[15,256]{1,0:T(8,128)S(1)} %stack.239), channel_id=1, replica_groups=mesh['row'=8,'pair'=4] {'row'}, use_global_device_ids=true, to_apply=%region_49.50 | all-reduce | flops 3840 | bytes 30720 | tf_op jit(solution)/shard_map/psum | solution.py:98
  221.9 2.6 fusion.200
  227.7 2.0 multiply_add_fusion.33
  232.4 5.0 %fusion.222 = (f32[256]{0:T(256)S(1)}, f32[256]{0:T(256)S(1)}, f32[256]{0:T(256)S(1)}, f32[256]{0:T(256)S(1)}, f32[256]{0:T(256)S(1)}, /*index=5*/f32[256]{0:T(256)S(1)}) fusion(f32[1]{0:T(128)} %slice.1126, f32[255]{0:T(256)S(1)} %slice.1125, f32[1]{0:T(128)} %slice.1116, f32[255]{0:T(256)S(1)} %slice.1115, f32[256]{0:T(256)S(1)} %get-tuple-element.174, ...), kind=kLoop, calls=%fused_computation.763 | loop fusion | flops 18176 | bytes 28672 | tf_op jit(solution)/shard_map/mul | solution.py:51
  237.4 2.5 multiply_add_fusion.31
  245.2 7.0 %add_rsqrt_fusion.7 = (f32[1,256]{1,0:T(1,128)S(1)}, f32[1,256]{1,0:T(1,128)S(1)}, f32[1,256]{1,0:T(1,128)S(1)}) fusion(f32[1,1]{1,0:T(1,128)} %bitcast.221, f32[1,255]{1,0:T(1,128)S(1)} %bitcast.657, f32[1,1]{1,0:T(1,128)} %bitcast.219, f32[1,255]{1,0:T(1,128)S(1)} %bitcast.661, f32[15,256]{1,0:T(8,128)S(1)} %psum.30, f32[1,3]{1,0:T(1,128)S(1)} %slice_bitcast_fusion.4, ...), kind=kLoop, calls=%fused_computation.598 | loop fusion | flops 30720 | bytes 34816 | tf_op jit(solution)/shard_map/sqrt | solution.py:50
  252.9 8.4 %collective-permute-start.4 = (f32[192,256]{1,0:T(8,128)S(1)}, f32[192,256]{1,0:T(8,128)S(1)}, u32[]{:S(2)}, u32[]{:S(2)}) collective-permute-start(f32[192,256]{1,0:T(8,128)S(1)} %get-tuple-element.160), channel_id=1, source_target_pairs={{0,1},{1,2},{2,3},{4,5},{5,6},{6,7},{8,9},{9,10},{10,11},{12,13},{... | collective-permute-start | bytes 589832 | tf_op jit(solution)/shard_map/ppermute | solution.py:14
  263.9 4.4 %collective-permute-done.5 = f32[192,256]{1,0:T(8,128)S(1)} collective-permute-done((f32[192,256]{1,0:T(8,128)S(1)}, f32[192,256]{1,0:T(8,128)S(1)}, u32[]{:S(2)}, u32[]{:S(2)}) %collective-permute-start.5) | collective-permute-done | bytes 196640 | tf_op jit(solution)/shard_map/ppermute | solution.py:14
  269.6 26.3 %psum.31 = f32[15,256]{1,0:T(8,128)S(1)} all-reduce(f32[15,256]{1,0:T(8,128)S(1)} %stack.255), channel_id=1, replica_groups=mesh['row'=8,'pair'=4] {'row'}, use_global_device_ids=true, to_apply=%region_65.66 | all-reduce | flops 3840 | bytes 30720 | tf_op jit(solution)/shard_map/psum | solution.py:98
  298.4 2.6 fusion.209
  304.2 2.0 multiply_add_fusion.18
  308.9 5.0 %fusion.224 = (f32[256]{0:T(256)S(1)}, f32[256]{0:T(256)S(1)}, f32[256]{0:T(256)S(1)}, f32[256]{0:T(256)S(1)}, f32[256]{0:T(256)S(1)}, /*index=5*/f32[256]{0:T(256)S(1)}) fusion(f32[1]{0:T(128)} %slice.1203, f32[255]{0:T(256)S(1)} %slice.1202, f32[1]{0:T(128)} %slice.1193, f32[255]{0:T(256)S(1)} %slice.1192, f32[256]{0:T(256)S(1)} %get-tuple-element.149, ...), kind=kLoop, calls=%fused_computation.765 | loop fusion | flops 18176 | bytes 28672 | tf_op jit(solution)/shard_map/mul | solution.py:51
  313.9 2.5 multiply_add_fusion.16
  321.7 7.0 %add_rsqrt_fusion = (f32[1,256]{1,0:T(1,128)S(1)}, f32[1,256]{1,0:T(1,128)S(1)}, f32[1,256]{1,0:T(1,128)S(1)}) fusion(f32[1,1]{1,0:T(1,128)} %bitcast.297, f32[1,255]{1,0:T(1,128)S(1)} %bitcast.658, f32[1,1]{1,0:T(1,128)} %bitcast.295, f32[1,255]{1,0:T(1,128)S(1)} %bitcast.662, f32[15,256]{1,0:T(8,128)S(1)} %psum.31, f32[1,3]{1,0:T(1,128)S(1)} %slice_bitcast_fusion, ...), kind=kLoop, calls=%fused_computation.553 | loop fusion | flops 30720 | bytes 34816 | tf_op jit(solution)/shard_map/sqrt | solution.py:50
  329.4 8.4 %collective-permute-start.6 = (f32[192,256]{1,0:T(8,128)S(1)}, f32[192,256]{1,0:T(8,128)S(1)}, u32[]{:S(2)}, u32[]{:S(2)}) collective-permute-start(f32[192,256]{1,0:T(8,128)S(1)} %get-tuple-element.135), channel_id=1, source_target_pairs={{0,1},{1,2},{2,3},{4,5},{5,6},{6,7},{8,9},{9,10},{10,11},{12,13},{... | collective-permute-start | bytes 589832 | tf_op jit(solution)/shard_map/ppermute | solution.py:14
  340.4 4.4 %collective-permute-done.7 = f32[192,256]{1,0:T(8,128)S(1)} collective-permute-done((f32[192,256]{1,0:T(8,128)S(1)}, f32[192,256]{1,0:T(8,128)S(1)}, u32[]{:S(2)}, u32[]{:S(2)}) %collective-permute-start.7) | collective-permute-done | bytes 196640 | tf_op jit(solution)/shard_map/ppermute | solution.py:14
  (333 shorter events, 80.6 us)
Async XLA Ops:
  6.5 24.6 %all-gather.2.cloned.1.call-start = ((), (), s32[]{:S(2)}) async-start(), calls=%async_computation | async-start | bytes 1966080 | tf_op jit(solution)/shard_map/all_gather | solution.py:89
  98.7 12.2 %collective-permute-start = (f32[192,256]{1,0:T(8,128)S(1)}, f32[192,256]{1,0:T(8,128)S(1)}, u32[]{:S(2)}, u32[]{:S(2)}) collective-permute-start(f32[192,256]{1,0:T(8,128)S(1)} %get-tuple-element.210), channel_id=1, source_target_pairs={{0,1},{1,2},{2,3},{4,5},{5,6},{6,7},{8,9},{9,10},{10,11},{12,13},{... | collective-permute-start | bytes 589832 | tf_op jit(solution)/shard_map/ppermute | solution.py:14
  108.3 7.0 %collective-permute-start.1 = (f32[192,256]{1,0:T(8,128)S(1)}, f32[192,256]{1,0:T(8,128)S(1)}, u32[]{:S(2)}, u32[]{:S(2)}) collective-permute-start(f32[192,256]{1,0:T(8,128)S(1)} %get-tuple-element.211), channel_id=1, source_target_pairs={{1,0},{2,1},{3,2},{5,4},{6,5},{7,6},{9,8},{10,9},{11,10},{13,12},{... | collective-permute-start | bytes 589832 | tf_op jit(solution)/shard_map/ppermute | solution.py:14
  176.4 11.0 %collective-permute-start.2 = (f32[192,256]{1,0:T(8,128)S(1)}, f32[192,256]{1,0:T(8,128)S(1)}, u32[]{:S(2)}, u32[]{:S(2)}) collective-permute-start(f32[192,256]{1,0:T(8,128)S(1)} %get-tuple-element.185), channel_id=1, source_target_pairs={{0,1},{1,2},{2,3},{4,5},{5,6},{6,7},{8,9},{9,10},{10,11},{12,13},{... | collective-permute-start | bytes 589832 | tf_op jit(solution)/shard_map/ppermute | solution.py:14
  184.8 7.0 %collective-permute-start.3 = (f32[192,256]{1,0:T(8,128)S(1)}, f32[192,256]{1,0:T(8,128)S(1)}, u32[]{:S(2)}, u32[]{:S(2)}) collective-permute-start(f32[192,256]{1,0:T(8,128)S(1)} %get-tuple-element.186), channel_id=1, source_target_pairs={{1,0},{2,1},{3,2},{5,4},{6,5},{7,6},{9,8},{10,9},{11,10},{13,12},{... | collective-permute-start | bytes 589832 | tf_op jit(solution)/shard_map/ppermute | solution.py:14
  252.9 11.0 %collective-permute-start.4 = (f32[192,256]{1,0:T(8,128)S(1)}, f32[192,256]{1,0:T(8,128)S(1)}, u32[]{:S(2)}, u32[]{:S(2)}) collective-permute-start(f32[192,256]{1,0:T(8,128)S(1)} %get-tuple-element.160), channel_id=1, source_target_pairs={{0,1},{1,2},{2,3},{4,5},{5,6},{6,7},{8,9},{9,10},{10,11},{12,13},{... | collective-permute-start | bytes 589832 | tf_op jit(solution)/shard_map/ppermute | solution.py:14
  261.3 7.0 %collective-permute-start.5 = (f32[192,256]{1,0:T(8,128)S(1)}, f32[192,256]{1,0:T(8,128)S(1)}, u32[]{:S(2)}, u32[]{:S(2)}) collective-permute-start(f32[192,256]{1,0:T(8,128)S(1)} %get-tuple-element.161), channel_id=1, source_target_pairs={{1,0},{2,1},{3,2},{5,4},{6,5},{7,6},{9,8},{10,9},{11,10},{13,12},{... | collective-permute-start | bytes 589832 | tf_op jit(solution)/shard_map/ppermute | solution.py:14
  329.4 11.0 %collective-permute-start.6 = (f32[192,256]{1,0:T(8,128)S(1)}, f32[192,256]{1,0:T(8,128)S(1)}, u32[]{:S(2)}, u32[]{:S(2)}) collective-permute-start(f32[192,256]{1,0:T(8,128)S(1)} %get-tuple-element.135), channel_id=1, source_target_pairs={{0,1},{1,2},{2,3},{4,5},{5,6},{6,7},{8,9},{9,10},{10,11},{12,13},{... | collective-permute-start | bytes 589832 | tf_op jit(solution)/shard_map/ppermute | solution.py:14
  337.8 7.0 %collective-permute-start.7 = (f32[192,256]{1,0:T(8,128)S(1)}, f32[192,256]{1,0:T(8,128)S(1)}, u32[]{:S(2)}, u32[]{:S(2)}) collective-permute-start(f32[192,256]{1,0:T(8,128)S(1)} %get-tuple-element.136), channel_id=1, source_target_pairs={{1,0},{2,1},{3,2},{5,4},{6,5},{7,6},{9,8},{10,9},{11,10},{13,12},{... | collective-permute-start | bytes 589832 | tf_op jit(solution)/shard_map/ppermute | solution.py:14
Sparse Core Ops, SparseCore 0:
  8.9 22.1 all-gather.1

commit v2 on v1

v2 whole, which is shorter than its diff:
```python
import functools

import jax
import jax.numpy as jnp
from jax import lax
from jax.experimental import pallas as pl
from jax.experimental.pallas import tpu as pltpu
from jax.sharding import PartitionSpec as P

B = 256
STEPS = 4
INNER = 4
TILE = 8
CHUNKS = 2
BANDS = 4 * INNER
MESH = pl.DeviceIdType.MESH


def ahead(values, distance):
    shift = (-distance) % B
    return pltpu.roll(values, shift, axis=1) if shift else values


def band_products(upper, lower):
    products = []
    for o in range(INNER):
        u, l = ahead(upper, o), ahead(lower, o)
        products += [upper * u, lower * l, upper * l]
        if o:
            products.append(lower * u)
    return products


def solve_bands(bands):
    uu, ll, ul, lu = {}, {}, {}, {}
    at = 0
    for o in range(INNER):
        uu[o], ll[o], ul[o] = bands[at], bands[at + 1], bands[at + 2]
        at += 3
        if o:
            lu[o] = bands[at]
            at += 1
    turns = []
    for sweep in range(INNER):
        differ = ll[0] - uu[0]
        coupling = ul[0]
        total = uu[0] + ll[0]
        signs = jnp.where(differ >= 0.0, 1.0, -1.0)
        denom = jnp.abs(differ) + jnp.sqrt(
            differ * differ + 4.0 * coupling * coupling + 1e-12 * (total * total)
        )
        tangent = 2.0 * signs * coupling / denom
        c = 1.0 / jnp.sqrt(1.0 + tangent * tangent)
        s = tangent * c
        turns.append((c, s))
        reach = INNER - 1 - sweep
        if reach == 0:
            break
        new_uu, new_ll, new_ul, new_lu = {}, {}, {}, {}
        for o in range(reach + 1):
            cj, sj = ahead(c, o), ahead(s, o)
            a, b, d = uu[o], ul[o], ll[o]
            e = lu[o] if o else ul[0]
            top_u, top_l = c * a - s * e, c * b - s * d
            low_u, low_l = s * a + c * e, s * b + c * d
            new_ul[o] = sj * top_u + cj * top_l
            if o < reach:
                new_uu[o] = cj * top_u - sj * top_l
                new_ll[o] = sj * low_u + cj * low_l
                if o:
                    new_lu[o] = cj * low_u - sj * low_l
        uu = new_uu
        ll = {o: ahead(new_ll[o], 1) for o in new_ll}
        ul = {o: new_ul[o + 1] for o in range(reach)}
        lu = {o: ahead(new_lu[o - 1] if o > 1 else new_ul[0], 1) for o in range(1, reach)}
    return turns


def turn(upper, lower, turns):
    for k, (c, s) in enumerate(turns):
        upper, lower = c * upper - s * lower, s * upper + c * lower
        if k < INNER - 1:
            lower = ahead(lower, 1)
    return upper, ahead(lower, 1 - INNER)


def kernel(
    nrow, npair, seat_ref, m_ref, out_ref, g, x, r, part,
    g_send, f_send, g_recv, p_send, p_recv, m_send, m_recv, own_sem,
):
    me = lax.axis_index("row")
    place = lax.axis_index("pair")
    height = m_ref.shape[0]
    chunk = height // CHUNKS
    core = lax.rem(place, 2)
    across = lax.div(place, 2)
    nacross = npair // 2
    sibling = 2 * across + 1 - core
    has_next = place < npair - 1
    has_prev = place > 0

    barrier = pltpu.get_barrier_semaphore()
    for d in range(1, npair):
        pl.semaphore_signal(
            barrier, inc=1, device_id=(me, lax.rem(place + d, npair)), device_id_type=MESH
        )
    for d in range(1, nrow):
        pl.semaphore_signal(
            barrier, inc=1, device_id=(lax.rem(me + d, nrow), place), device_id_type=MESH
        )
    pl.semaphore_wait(barrier, npair + nrow - 2)

    def remote(src, dst, send, recv, device):
        return pltpu.make_async_remote_copy(
            src_ref=src, dst_ref=dst, send_sem=send, recv_sem=recv,
            device_id=device, device_id_type=MESH,
        )

    def columns(b):
        return m_ref.at[:, pl.ds(b * B, B)]

    def direct(d, b):
        target = sibling if d == 0 else 2 * lax.rem(across + d, nacross) + core
        slot = 2 * place + b
        return remote(columns(b), g.at[slot], g_send.at[d, b], g_recv.at[slot], (me, target))

    def forward(d, b):
        slot = 2 * (2 * lax.rem(across + d, nacross) + core) + b
        return remote(g.at[slot], g.at[slot], f_send.at[d, b], g_recv.at[slot], (me, sibling))

    for b in range(2):
        for d in range(1, nacross):
            direct(d, b).start()
    for b in range(2):
        direct(0, b).start()
    own = [
        pltpu.make_async_copy(columns(b), g.at[2 * place + b], own_sem.at[b]) for b in range(2)
    ]
    for copy in own:
        copy.start()
    for b in range(2):
        for d in range(1, nacross):
            forward(d, b).wait_recv()
            forward(d, b).start()
    for copy in own:
        copy.wait()
    for b in range(2):
        for d in range(nacross):
            slot = 2 * (2 * lax.rem(across + d, nacross) + 1 - core) + b
            remote(
                g.at[slot], g.at[slot], f_send.at[0, b], g_recv.at[slot], (me, sibling)
            ).wait_recv()

    first = seat_ref[2 * place]
    second = seat_ref[2 * place + 1]

    @pl.loop(0, height // TILE)
    def seat(t):
        rows = pl.ds(t * TILE, TILE)
        x[0, 0, rows, :] = g[first, rows, :]
        x[0, 1, rows, :] = g[second, rows, :]

    def partial_copy(s, d):
        return remote(
            part.at[s, me], part.at[s, me], p_send.at[s, d], p_recv.at[s, me],
            (lax.rem(me + d, nrow), place),
        )

    def move(s, way, c):
        rows = pl.ds(c * chunk, chunk)
        if way == 0:
            src = r.at[s, jnp.where(has_prev, 0, 1), rows]
            target = lax.rem(place + 1, npair)
        else:
            src = r.at[s, 1, rows]
            target = lax.rem(place + npair - 1, npair)
        return remote(
            src, x.at[s + 1, way, rows], m_send.at[s, way, c], m_recv.at[s, way, c], (me, target)
        )

    def arrived(s, c):
        @pl.when(has_prev)
        def _():
            move(s, 0, c).wait_recv()

        @pl.when(has_next)
        def _():
            move(s, 1, c).wait_recv()

    kept = jnp.where(has_prev, jnp.where(has_next, 2, 1), 0)

    @pl.loop(0, STEPS)
    def step(s):
        sums = tuple(jnp.zeros((TILE, B), jnp.float32) for _ in range(BANDS - 1))
        for c in range(CHUNKS):
            @pl.when(s > 0)
            def _():
                arrived(s - 1, c)

            def add(t, totals):
                rows = pl.ds(c * chunk + t * TILE, TILE)
                products = band_products(x[s, 0, rows, :], x[s, 1, rows, :])
                return tuple(a + b for a, b in zip(totals, products))

            sums = lax.fori_loop(0, chunk // TILE, add, sums)
        for k in range(BANDS - 1):
            part[s, me, k:k + 1, :] = jnp.sum(sums[k], axis=0, keepdims=True)
        part[s, me, BANDS - 1:BANDS, :] = jnp.zeros((1, B), jnp.float32)
        for d in range(1, nrow):
            partial_copy(s, d).start()
        for d in range(1, nrow):
            source = lax.rem(me + d, nrow)
            remote(
                part.at[s, source], part.at[s, source], p_send.at[s, d], p_recv.at[s, source],
                (source, place),
            ).wait_recv()
        whole = part[s, 0]
        for k in range(1, nrow):
            whole = whole + part[s, k]
        bands = [jnp.broadcast_to(whole[k:k + 1, :], (TILE, B)) for k in range(BANDS - 1)]
        turns = solve_bands(bands)
        for c in range(CHUNKS):
            @pl.loop(0, chunk // TILE)
            def rotate(t):
                rows = pl.ds(c * chunk + t * TILE, TILE)
                upper, lower = turn(x[s, 0, rows, :], x[s, 1, rows, :], turns)
                r[s, 0, rows, :] = upper
                r[s, 1, rows, :] = lower
                x[s + 1, kept, rows, :] = upper

            @pl.when(has_next)
            def _():
                move(s, 0, c).start()

            @pl.when(has_prev)
            def _():
                move(s, 1, c).start()

    for c in range(CHUNKS):
        arrived(STEPS - 1, c)

        @pl.loop(0, chunk // TILE)
        def hand_out(t):
            rows = pl.ds(c * chunk + t * TILE, TILE)
            out_ref[rows, 0:B] = x[STEPS, 0, rows, :]
            out_ref[rows, B:2 * B] = x[STEPS, 1, rows, :]

    for b in range(2):
        for d in range(nacross):
            direct(d, b).wait_send()
            if d:
                forward(d, b).wait_send()

    @pl.loop(0, STEPS)
    def drain(s):
        for d in range(1, nrow):
            partial_copy(s, d).wait_send()
        for c in range(CHUNKS):
            @pl.when(has_next)
            def _():
                move(s, 0, c).wait_send()

            @pl.when(has_prev)
            def _():
                move(s, 1, c).wait_send()


def local(nrow, npair, matrix, seating):
    height = matrix.shape[0]
    nacross = npair // 2
    dma = pltpu.SemaphoreType.DMA
    return pl.pallas_call(
        functools.partial(kernel, nrow, npair),
        out_shape=jax.ShapeDtypeStruct(matrix.shape, jnp.float32),
        in_specs=[
            pl.BlockSpec(memory_space=pltpu.SMEM),
            pl.BlockSpec(memory_space=pltpu.VMEM),
        ],
        out_specs=pl.BlockSpec(memory_space=pltpu.VMEM),
        scratch_shapes=[
            pltpu.VMEM((2 * npair, height, B), jnp.float32),
            pltpu.VMEM((STEPS + 1, 3, height, B), jnp.float32),
            pltpu.VMEM((STEPS, 2, height, B), jnp.float32),
            pltpu.VMEM((STEPS, nrow, BANDS, B), jnp.float32),
            dma((nacross, 2)),
            dma((nacross, 2)),
            dma((2 * npair,)),
            dma((STEPS, nrow)),
            dma((STEPS, nrow)),
            dma((STEPS, 2, CHUNKS)),
            dma((STEPS, 2, CHUNKS)),
            dma((2,)),
        ],
        compiler_params=pltpu.CompilerParams(
            collective_id=0, has_side_effects=True, vmem_limit_bytes=32 * 1024 * 1024
        ),
    )(seating, matrix)


def solution(mesh):
    sizes = dict(mesh.shape)
    return jax.shard_map(
        functools.partial(local, sizes["row"], sizes["pair"]),
        mesh=mesh, in_specs=(P("row", "pair"), P()), out_specs=P("row", "pair"), check_vma=False,
    )
```

time: 354 us -> 85.6 us (0.24)
  blocking collectives: 109 us -> 0 us
  other arithmetic: 98.1 us -> 0 us
  Pallas kernels: 0 us -> 83.1 us
  local copies, waits for them, and re-layouts: 46.4 us -> 2.4 us
  starting transfers between devices: 42.5 us -> 0 us
  waiting for transfers between devices: 42.2 us -> 0 us
  between operations: 14.5 us -> 0.01 us
    psum x4 -> x0, blocking collectives: 109 us -> none  [local(): bands = lax.psum(band_sums(upper, lower), 'row')]
    pallas_call x0 -> x1, Pallas kernels: none -> 83.1 us  [local(): pl.pallas_call(functools.partial(kernel, nrow, npair), out_shape=jax.Shap...]
    slice x225 -> x0, local copies, waits for them, and re-layouts: 43.4 us -> none  [the longest x220 42.8 us: ahead(): return jnp.roll(values, -distance, axis=-1) if distance else values]
    ppermute x8 -> x0, starting transfers between devices: 42.5 us -> none  [shifted(): return lax.ppermute(block, axis, route)]
    sqrt x8 -> x0, other arithmetic: 28 us -> none  [solve_bands(): c = 1.0 / jnp.sqrt(1.0 + tangent * tangent)]
    mul x12 -> x0, other arithmetic: 23.3 us -> none  [solve_bands(): s = tangent * c]
    add x40 -> x0, other arithmetic: 22.8 us -> none  [the longest x16 13 us: solve_bands(): new_ll[o] = sj * low_u + cj * low_l]
    all_gather x1 -> x0, waiting for transfers between devices: 21.3 us -> none  [local(): piece = lax.all_gather(matrix, 'pair', axis=1, tiled=True)]
  transfers between devices with their start and end apart: 9 -> 0, of which waited for: 9 -> 0; matrix products, arithmetic and copies ran while one was open for 1% -> 0% of each run, Pallas kernels for 0% -> 0%
where the time goes in v2:
time: 85.6 us; the launch traced here: 85.5 us
  Pallas kernels  83.1 us (97%)
  local copies, waits for them, and re-layouts  2.4 us (3%)
    pallas_call x1, Pallas kernels, local(): pl.pallas_call(functools.partial(kernel, nrow, npair), out_shape=jax.Shap...  83.1 us
    unnamed x5, local copies, waits for them, and re-layouts  2.4 us

profile of v2, /device:TPU:1, one launch (start us, length us, event | category | flops | bytes accessed | tf_op | source)
XLA Modules:
  0.0 85.5 jit_solution(1427877005210471215)
XLA Ops:
  0.0 0.0 copy-start
  0.0 1.0 %copy-done = f32[192,512]{1,0:T(8,128)S(1)} copy-done((f32[192,512]{1,0:T(8,128)S(1)}, f32[192,512]{1,0:T(8,128)}, u32[]{:S(2)}) %copy-start) | copy-done | bytes 393240
  1.0 0.0 copy-start.1
  1.0 0.7 copy-done.1
  1.7 83.1 %shard_map.28 = f32[192,512]{1,0:T(8,128)S(1)} custom-call(s32[8]{0:T(128)S(1)} %copy-done.1, f32[192,512]{1,0:T(8,128)S(1)} %copy-done), custom_call_target="tpu_custom_call" | custom-call | tf_op jit(solution)/shard_map/pallas_call | solution.py:272
  84.7 0.7 copy.4
Async XLA Ops:
  0.0 1.0 %copy-start = (f32[192,512]{1,0:T(8,128)S(1)}, f32[192,512]{1,0:T(8,128)}, u32[]{:S(2)}) copy-start(f32[192,512]{1,0:T(8,128)} %m_ref.1) | copy-start | bytes 1179652
  1.0 0.7 copy-start.1

commit v3 on v2

--- a/solution.py
+++ b/solution.py
@@ -11,6 +11,7 @@
 STEPS = 4
 INNER = 4
 TILE = 8
+GROUP = 4
 CHUNKS = 2
 BANDS = 4 * INNER
 MESH = pl.DeviceIdType.MESH
@@ -50,7 +51,7 @@
             differ * differ + 4.0 * coupling * coupling + 1e-12 * (total * total)
         )
         tangent = 2.0 * signs * coupling / denom
-        c = 1.0 / jnp.sqrt(1.0 + tangent * tangent)
+        c = lax.rsqrt(1.0 + tangent * tangent)
         s = tangent * c
         turns.append((c, s))
         reach = INNER - 1 - sweep
@@ -76,17 +77,17 @@
     return turns
 
 
-def turn(upper, lower, turns):
+def turn(pairs, turns):
     for k, (c, s) in enumerate(turns):
-        upper, lower = c * upper - s * lower, s * upper + c * lower
-        if k < INNER - 1:
-            lower = ahead(lower, 1)
-    return upper, ahead(lower, 1 - INNER)
+        pairs = [(c * u - s * l, s * u + c * l) for u, l in pairs]
+        distance = 1 if k < INNER - 1 else 1 - INNER
+        pairs = [(u, ahead(l, distance)) for u, l in pairs]
+    return pairs
 
 
 def kernel(
-    nrow, npair, seat_ref, m_ref, out_ref, g, x, r, part,
-    g_send, f_send, g_recv, p_send, p_recv, m_send, m_recv, own_sem,
+    nrow, npair, seating_ref, m_ref, out_ref, seat_ref, g, x, r, part,
+    g_send, f_send, g_recv, p_send, p_recv, m_send, m_recv, own_sem, seat_sem,
 ):
     me = lax.axis_index("row")
     place = lax.axis_index("pair")
@@ -133,6 +134,8 @@
             direct(d, b).start()
     for b in range(2):
         direct(0, b).start()
+    seats = pltpu.make_async_copy(seating_ref, seat_ref, seat_sem)
+    seats.start()
     own = [
         pltpu.make_async_copy(columns(b), g.at[2 * place + b], own_sem.at[b]) for b in range(2)
     ]
@@ -151,14 +154,20 @@
                 g.at[slot], g.at[slot], f_send.at[0, b], g_recv.at[slot], (me, sibling)
             ).wait_recv()
 
+    seats.wait()
     first = seat_ref[2 * place]
     second = seat_ref[2 * place + 1]
 
-    @pl.loop(0, height // TILE)
-    def seat(t):
-        rows = pl.ds(t * TILE, TILE)
-        x[0, 0, rows, :] = g[first, rows, :]
-        x[0, 1, rows, :] = g[second, rows, :]
+    def tiles(c, t):
+        start = c * chunk + t * (TILE * GROUP)
+        return [pl.ds(start + i * TILE, TILE) for i in range(GROUP)]
+
+    for c in range(CHUNKS):
+        @pl.loop(0, chunk // (TILE * GROUP))
+        def seat(t):
+            for rows in tiles(c, t):
+                x[0, 0, rows, :] = g[first, rows, :]
+                x[0, 1, rows, :] = g[second, rows, :]
 
     def partial_copy(s, d):
         return remote(
@@ -198,11 +207,12 @@
                 arrived(s - 1, c)
 
             def add(t, totals):
-                rows = pl.ds(c * chunk + t * TILE, TILE)
-                products = band_products(x[s, 0, rows, :], x[s, 1, rows, :])
-                return tuple(a + b for a, b in zip(totals, products))
-
-            sums = lax.fori_loop(0, chunk // TILE, add, sums)
+                for rows in tiles(c, t):
+                    products = band_products(x[s, 0, rows, :], x[s, 1, rows, :])
+                    totals = tuple(a + b for a, b in zip(totals, products))
+                return totals
+
+            sums = lax.fori_loop(0, chunk // (TILE * GROUP), add, sums)
         for k in range(BANDS - 1):
             part[s, me, k:k + 1, :] = jnp.sum(sums[k], axis=0, keepdims=True)
         part[s, me, BANDS - 1:BANDS, :] = jnp.zeros((1, B), jnp.float32)
@@ -220,13 +230,14 @@
         bands = [jnp.broadcast_to(whole[k:k + 1, :], (TILE, B)) for k in range(BANDS - 1)]
         turns = solve_bands(bands)
         for c in range(CHUNKS):
-            @pl.loop(0, chunk // TILE)
+            @pl.loop(0, chunk // (TILE * GROUP))
             def rotate(t):
-                rows = pl.ds(c * chunk + t * TILE, TILE)
-                upper, lower = turn(x[s, 0, rows, :], x[s, 1, rows, :], turns)
-                r[s, 0, rows, :] = upper
-                r[s, 1, rows, :] = lower
-                x[s + 1, kept, rows, :] = upper
+                held = tiles(c, t)
+                pairs = turn([(x[s, 0, rows, :], x[s, 1, rows, :]) for rows in held], turns)
+                for rows, (upper, lower) in zip(held, pairs):
+                    r[s, 0, rows, :] = upper
+                    r[s, 1, rows, :] = lower
+                    x[s + 1, kept, rows, :] = upper
 
             @pl.when(has_next)
             def _():
@@ -239,11 +250,11 @@
     for c in range(CHUNKS):
         arrived(STEPS - 1, c)
 
-        @pl.loop(0, chunk // TILE)
+        @pl.loop(0, chunk // (TILE * GROUP))
         def hand_out(t):
-            rows = pl.ds(c * chunk + t * TILE, TILE)
-            out_ref[rows, 0:B] = x[STEPS, 0, rows, :]
-            out_ref[rows, B:2 * B] = x[STEPS, 1, rows, :]
+            for rows in tiles(c, t):
+                out_ref[rows, 0:B] = x[STEPS, 0, rows, :]
+                out_ref[rows, B:2 * B] = x[STEPS, 1, rows, :]
 
     for b in range(2):
         for d in range(nacross):
@@ -273,11 +284,12 @@
         functools.partial(kernel, nrow, npair),
         out_shape=jax.ShapeDtypeStruct(matrix.shape, jnp.float32),
         in_specs=[
-            pl.BlockSpec(memory_space=pltpu.SMEM),
-            pl.BlockSpec(memory_space=pltpu.VMEM),
+            pl.BlockSpec(memory_space=pltpu.HBM),
+            pl.BlockSpec(memory_space=pltpu.HBM),
         ],
         out_specs=pl.BlockSpec(memory_space=pltpu.VMEM),
         scratch_shapes=[
+            pltpu.SMEM((2 * npair,), jnp.int32),
             pltpu.VMEM((2 * npair, height, B), jnp.float32),
             pltpu.VMEM((STEPS + 1, 3, height, B), jnp.float32),
             pltpu.VMEM((STEPS, 2, height, B), jnp.float32),
@@ -290,6 +302,7 @@
             dma((STEPS, 2, CHUNKS)),
             dma((STEPS, 2, CHUNKS)),
             dma((2,)),
+            dma,
         ],
         compiler_params=pltpu.CompilerParams(
             collective_id=0, has_side_effects=True, vmem_limit_bytes=32 * 1024 * 1024

time: 85.6 us -> 61.9 us (0.72)
  Pallas kernels: 83.1 us -> 59.3 us
    pallas_call x1, Pallas kernels: 83.1 us -> 59.3 us  [local(): pl.pallas_call(functools.partial(kernel, nrow, npair), out_shape=jax.Shap...]
where the time goes in v3:
time: 61.9 us; the launch traced here: 61.7 us
  Pallas kernels  59.3 us (96%)
  local copies, waits for them, and re-layouts  2.4 us (4%)
    pallas_call x1, Pallas kernels, local(): pl.pallas_call(functools.partial(kernel, nrow, npair), out_shape=jax.Shap...  59.3 us
    unnamed x5, local copies, waits for them, and re-layouts  2.4 us

profile of v3, /device:TPU:1, one launch (start us, length us, event | category | flops | bytes accessed | tf_op | source)
XLA Modules:
  0.0 61.7 jit_solution(17183163838027533505)
XLA Ops:
  0.0 0.0 copy-start
  0.0 1.0 %copy-done = f32[192,512]{1,0:T(8,128)S(1)} copy-done((f32[192,512]{1,0:T(8,128)S(1)}, f32[192,512]{1,0:T(8,128)}, u32[]{:S(2)}) %copy-start) | copy-done | bytes 393240
  1.0 0.0 copy-start.1
  1.0 0.7 %copy-done.1 = s32[8]{0:T(128)S(1)} copy-done((s32[8]{0:T(128)S(1)}, s32[8]{0:T(128)}, u32[]{:S(2)}) %copy-start.1) | copy-done | bytes 56
  1.7 59.3 %shard_map.28 = f32[192,512]{1,0:T(8,128)S(1)} custom-call(s32[8]{0:T(128)S(1)} %copy-done.1, f32[192,512]{1,0:T(8,128)S(1)} %copy-done), custom_call_target="tpu_custom_call" | custom-call | tf_op jit(solution)/shard_map/pallas_call | solution.py:283
  60.9 0.7 %copy.4 = f32[192,512]{1,0:T(8,128)} copy(f32[192,512]{1,0:T(8,128)S(1)} %shard_map.28) | data formatting | bytes 786432
Async XLA Ops:
  0.0 1.0 %copy-start = (f32[192,512]{1,0:T(8,128)S(1)}, f32[192,512]{1,0:T(8,128)}, u32[]{:S(2)}) copy-start(f32[192,512]{1,0:T(8,128)} %m_ref.1) | copy-start | bytes 1179652
  1.0 0.7 %copy-start.1 = (s32[8]{0:T(128)S(1)}, s32[8]{0:T(128)}, u32[]{:S(2)}) copy-start(s32[8]{0:T(128)} %seating_ref.1) | copy-start | bytes 100

commit v4 on v3

--- a/solution.py
+++ b/solution.py
@@ -12,7 +12,7 @@
 INNER = 4
 TILE = 8
 GROUP = 4
-CHUNKS = 2
+CHUNKS = 6
 BANDS = 4 * INNER
 MESH = pl.DeviceIdType.MESH
 
@@ -305,7 +305,7 @@
             dma,
         ],
         compiler_params=pltpu.CompilerParams(
-            collective_id=0, has_side_effects=True, vmem_limit_bytes=32 * 1024 * 1024
+            collective_id=0, has_side_effects=True, vmem_limit_bytes=60 * 1024 * 1024
         ),
     )(seating, matrix)
 

time: 61.9 us -> 58.7 us (0.948)
  Pallas kernels: 59.3 us -> 56.8 us
  local copies, waits for them, and re-layouts: 2.4 us -> 1.77 us
    pallas_call x1, Pallas kernels: 59.3 us -> 56.8 us  [local(): pl.pallas_call(functools.partial(kernel, nrow, npair), out_shape=jax.Shap...]
    unnamed x5 -> x1, local copies, waits for them, and re-layouts: 2.4 us -> 1.77 us
where the time goes in v4:
time: 58.7 us; the launch traced here: 58.6 us
  Pallas kernels  56.8 us (97%)
  local copies, waits for them, and re-layouts  1.77 us (3%)
    pallas_call x1, Pallas kernels, local(): pl.pallas_call(functools.partial(kernel, nrow, npair), out_shape=jax.Shap...  56.8 us
    unnamed x1, local copies, waits for them, and re-layouts  1.77 us

profile of v4, /device:TPU:1, one launch (start us, length us, event | category | flops | bytes accessed | tf_op | source)
XLA Modules:
  0.0 58.6 jit_solution(4933714712821253739)
XLA Ops:
  0.0 56.8 %shard_map.28 = f32[192,512]{1,0:T(8,128)} custom-call(s32[8]{0:T(128)} %seating_ref.1, f32[192,512]{1,0:T(8,128)} %m_ref.1), custom_call_target="tpu_custom_call" | custom-call | tf_op jit(solution)/shard_map/pallas_call | solution.py:283
  56.8 1.8 %copy.4 = f32[192,512]{1,0:T(8,128)} copy(f32[192,512]{1,0:T(8,128)} %shard_map.28) | data formatting | bytes 786432

commit v5 on v4

--- a/solution.py
+++ b/solution.py
@@ -14,6 +14,7 @@
 GROUP = 4
 CHUNKS = 6
 BANDS = 4 * INNER
+LANES = 128
 MESH = pl.DeviceIdType.MESH
 
 
@@ -86,13 +87,14 @@
 
 
 def kernel(
-    nrow, npair, seating_ref, m_ref, out_ref, seat_ref, g, x, r, part,
-    g_send, f_send, g_recv, p_send, p_recv, m_send, m_recv, own_sem, seat_sem,
+    nrow, npair, seating_ref, m_ref, out_ref, seat_ref, g, x, r, part, shares, summed,
+    g_send, f_send, g_recv, p_send, p_recv, q_send, q_recv, m_send, m_recv, own_sem, seat_sem,
 ):
     me = lax.axis_index("row")
     place = lax.axis_index("pair")
     height = m_ref.shape[0]
     chunk = height // CHUNKS
+    lines = BANDS * B // LANES // nrow
     core = lax.rem(place, 2)
     across = lax.div(place, 2)
     nacross = npair // 2
@@ -169,10 +171,23 @@
                 x[0, 0, rows, :] = g[first, rows, :]
                 x[0, 1, rows, :] = g[second, rows, :]
 
-    def partial_copy(s, d):
+    def share_copy(s, d):
+        peer = lax.rem(me + d, nrow)
         return remote(
-            part.at[s, me], part.at[s, me], p_send.at[s, d], p_recv.at[s, me],
+            part.at[s, peer], shares.at[s, d], p_send.at[s, d], p_recv.at[s, d], (peer, place)
+        )
+
+    def sum_copy(s, d):
+        return remote(
+            summed.at[s, me], summed.at[s, me], q_send.at[s, d], q_recv.at[s, me],
             (lax.rem(me + d, nrow), place),
+        )
+
+    def sum_from(s, d):
+        source = lax.rem(me + d, nrow)
+        return remote(
+            summed.at[s, source], summed.at[s, source], q_send.at[s, d], q_recv.at[s, source],
+            (source, place),
         )
 
     def move(s, way, c):
@@ -213,21 +228,31 @@
                 return totals
 
             sums = lax.fori_loop(0, chunk // (TILE * GROUP), add, sums)
+        for k in range(BANDS):
+            total = jnp.sum(sums[k], axis=0, keepdims=True) if k < BANDS - 1 else jnp.zeros((1, B))
+            for h in range(2):
+                at = 2 * k + h
+                part[s, at // lines, at % lines:at % lines + 1, :] = total[:, h * LANES:(h + 1) * LANES]
+        for d in range(1, nrow):
+            share_copy(s, d).start()
+        whole = part[s, me]
+        for d in range(1, nrow):
+            share_copy(s, d).wait_recv()
+        for d in range(1, nrow):
+            whole = whole + shares[s, d]
+        summed[s, me] = whole
+        for d in range(1, nrow):
+            sum_copy(s, d).start()
+        for d in range(1, nrow):
+            sum_from(s, d).wait_recv()
+        bands = []
         for k in range(BANDS - 1):
-            part[s, me, k:k + 1, :] = jnp.sum(sums[k], axis=0, keepdims=True)
-        part[s, me, BANDS - 1:BANDS, :] = jnp.zeros((1, B), jnp.float32)
-        for d in range(1, nrow):
-            partial_copy(s, d).start()
-        for d in range(1, nrow):
-            source = lax.rem(me + d, nrow)
-            remote(
-                part.at[s, source], part.at[s, source], p_send.at[s, d], p_recv.at[s, source],
-                (source, place),
-            ).wait_recv()
-        whole = part[s, 0]
-        for k in range(1, nrow):
-            whole = whole + part[s, k]
-        bands = [jnp.broadcast_to(whole[k:k + 1, :], (TILE, B)) for k in range(BANDS - 1)]
+            halves = []
+            for h in range(2):
+                at = 2 * k + h
+                line = summed[s, at // lines, at % lines:at % lines + 1, :]
+                halves.append(jnp.broadcast_to(line, (TILE, LANES)))
+            bands.append(jnp.concatenate(halves, axis=1))
         turns = solve_bands(bands)
         for c in range(CHUNKS):
             @pl.loop(0, chunk // (TILE * GROUP))
@@ -265,7 +290,8 @@
     @pl.loop(0, STEPS)
     def drain(s):
         for d in range(1, nrow):
-            partial_copy(s, d).wait_send()
+            share_copy(s, d).wait_send()
+            sum_copy(s, d).wait_send()
         for c in range(CHUNKS):
             @pl.when(has_next)
             def _():
@@ -279,6 +305,7 @@
 def local(nrow, npair, matrix, seating):
     height = matrix.shape[0]
     nacross = npair // 2
+    lines = BANDS * B // LANES // nrow
     dma = pltpu.SemaphoreType.DMA
     return pl.pallas_call(
         functools.partial(kernel, nrow, npair),
@@ -293,10 +320,14 @@
             pltpu.VMEM((2 * npair, height, B), jnp.float32),
             pltpu.VMEM((STEPS + 1, 3, height, B), jnp.float32),
             pltpu.VMEM((STEPS, 2, height, B), jnp.float32),
-            pltpu.VMEM((STEPS, nrow, BANDS, B), jnp.float32),
+            pltpu.VMEM((STEPS, nrow, lines, LANES), jnp.float32),
+            pltpu.VMEM((STEPS, nrow, lines, LANES), jnp.float32),
+            pltpu.VMEM((STEPS, nrow, lines, LANES), jnp.float32),
             dma((nacross, 2)),
             dma((nacross, 2)),
             dma((2 * npair,)),
+            dma((STEPS, nrow)),
+            dma((STEPS, nrow)),
             dma((STEPS, nrow)),
             dma((STEPS, nrow)),
             dma((STEPS, 2, CHUNKS)),

time: 58.7 us -> 71 us (1.21)
  Pallas kernels: 56.8 us -> 69.1 us
    pallas_call x1, Pallas kernels: 56.8 us -> 69.1 us  [local(): pl.pallas_call(functools.partial(kernel, nrow, npair), out_shape=jax.Shap...]
where the time goes in v5:
time: 71 us; the launch traced here: 70.8 us
  Pallas kernels  69.1 us (97%)
  local copies, waits for them, and re-layouts  1.77 us (2%)
    pallas_call x1, Pallas kernels, local(): pl.pallas_call(functools.partial(kernel, nrow, npair), out_shape=jax.Shap...  69.1 us
    unnamed x1, local copies, waits for them, and re-layouts  1.77 us

profile of v5, /device:TPU:1, one launch (start us, length us, event | category | flops | bytes accessed | tf_op | source)
XLA Modules:
  0.0 70.8 jit_solution(7615011811765142926)
XLA Ops:
  0.0 69.1 %shard_map.28 = f32[192,512]{1,0:T(8,128)} custom-call(s32[8]{0:T(128)} %seating_ref.1, f32[192,512]{1,0:T(8,128)} %m_ref.1), custom_call_target="tpu_custom_call" | custom-call | tf_op jit(solution)/shard_map/pallas_call | solution.py:310
  69.1 1.8 %copy.4 = f32[192,512]{1,0:T(8,128)} copy(f32[192,512]{1,0:T(8,128)} %shard_map.28) | data formatting | bytes 786432

commit v6 on v4

--- a/solution.py
+++ b/solution.py
@@ -13,6 +13,7 @@
 TILE = 8
 GROUP = 4
 CHUNKS = 6
+PARTS = 3
 BANDS = 4 * INNER
 MESH = pl.DeviceIdType.MESH
 
@@ -86,9 +87,10 @@
 
 
 def kernel(
-    nrow, npair, seating_ref, m_ref, out_ref, seat_ref, g, x, r, part,
-    g_send, f_send, g_recv, p_send, p_recv, m_send, m_recv, own_sem, seat_sem,
+    nrow, npair, seating_ref, m_ref, out_ref, seat_ref, *rest
 ):
+    g, rest = rest[:PARTS], rest[PARTS:]
+    (x, r, part, g_send, f_send, g_recv, p_send, p_recv, m_send, m_recv, own_sem, seat_sem) = rest
     me = lax.axis_index("row")
     place = lax.axis_index("pair")
     height = m_ref.shape[0]
@@ -117,43 +119,38 @@
             device_id=device, device_id_type=MESH,
         )
 
-    def columns(b):
-        return m_ref.at[:, pl.ds(b * B, B)]
-
-    def direct(d, b):
+    part_rows = height // PARTS
+
+    def columns(b, q):
+        return m_ref.at[pl.ds(q * part_rows, part_rows), pl.ds(b * B, B)]
+
+    def held(slot, q):
+        return g[q].at[slot]
+
+    def direct(d, b, q):
         target = sibling if d == 0 else 2 * lax.rem(across + d, nacross) + core
         slot = 2 * place + b
-        return remote(columns(b), g.at[slot], g_send.at[d, b], g_recv.at[slot], (me, target))
-
-    def forward(d, b):
-        slot = 2 * (2 * lax.rem(across + d, nacross) + core) + b
-        return remote(g.at[slot], g.at[slot], f_send.at[d, b], g_recv.at[slot], (me, sibling))
-
-    for b in range(2):
-        for d in range(1, nacross):
-            direct(d, b).start()
-    for b in range(2):
-        direct(0, b).start()
+        return remote(
+            columns(b, q), held(slot, q), g_send.at[d, b, q], g_recv.at[slot, q], (me, target)
+        )
+
+    def passed_on(d, b, q, owner_core):
+        slot = 2 * (2 * lax.rem(across + d, nacross) + owner_core) + b
+        return remote(
+            held(slot, q), held(slot, q), f_send.at[d, b, q], g_recv.at[slot, q], (me, sibling)
+        )
+
+    def own(b, q):
+        return pltpu.make_async_copy(columns(b, q), held(2 * place + b, q), own_sem.at[b, q])
+
     seats = pltpu.make_async_copy(seating_ref, seat_ref, seat_sem)
     seats.start()
-    own = [
-        pltpu.make_async_copy(columns(b), g.at[2 * place + b], own_sem.at[b]) for b in range(2)
-    ]
-    for copy in own:
-        copy.start()
-    for b in range(2):
-        for d in range(1, nacross):
-            forward(d, b).wait_recv()
-            forward(d, b).start()
-    for copy in own:
-        copy.wait()
-    for b in range(2):
-        for d in range(nacross):
-            slot = 2 * (2 * lax.rem(across + d, nacross) + 1 - core) + b
-            remote(
-                g.at[slot], g.at[slot], f_send.at[0, b], g_recv.at[slot], (me, sibling)
-            ).wait_recv()
-
+    for q in range(PARTS):
+        for b in range(2):
+            for d in range(1, nacross):
+                direct(d, b, q).start()
+            direct(0, b, q).start()
+            own(b, q).start()
     seats.wait()
     first = seat_ref[2 * place]
     second = seat_ref[2 * place + 1]
@@ -162,17 +159,35 @@
         start = c * chunk + t * (TILE * GROUP)
         return [pl.ds(start + i * TILE, TILE) for i in range(GROUP)]
 
-    for c in range(CHUNKS):
-        @pl.loop(0, chunk // (TILE * GROUP))
-        def seat(t):
-            for rows in tiles(c, t):
-                x[0, 0, rows, :] = g[first, rows, :]
-                x[0, 1, rows, :] = g[second, rows, :]
+    def gathered(q):
+        for b in range(2):
+            for d in range(1, nacross):
+                passed_on(d, b, q, core).wait_recv()
+                passed_on(d, b, q, core).start()
+        for b in range(2):
+            own(b, q).wait()
+            for d in range(nacross):
+                passed_on(d, b, q, 1 - core).wait_recv()
+        each = CHUNKS // PARTS
+        for c in range(q * each, (q + 1) * each):
+            @pl.loop(0, chunk // (TILE * GROUP))
+            def seat(t):
+                for rows, within in zip(tiles(c, t), tiles(c - q * each, t)):
+                    x[0, 0, rows, :] = g[q][first, within, :]
+                    x[0, 1, rows, :] = g[q][second, within, :]
+
+    def peer(d):
+        down = nrow - d
+        up = d - 1
+        return jnp.where(
+            2 * me < nrow,
+            jnp.where(down <= me, down - 1, down),
+            jnp.where(up >= me, up + 1, up),
+        )
 
     def partial_copy(s, d):
         return remote(
-            part.at[s, me], part.at[s, me], p_send.at[s, d], p_recv.at[s, me],
-            (lax.rem(me + d, nrow), place),
+            part.at[s, me], part.at[s, me], p_send.at[s, d], p_recv.at[s, me], (peer(d), place)
         )
 
     def move(s, way, c):
@@ -206,6 +221,11 @@
             def _():
                 arrived(s - 1, c)
 
+            if c % (CHUNKS // PARTS) == 0:
+                @pl.when(s == 0)
+                def _():
+                    gathered(c // (CHUNKS // PARTS))
+
             def add(t, totals):
                 for rows in tiles(c, t):
                     products = band_products(x[s, 0, rows, :], x[s, 1, rows, :])
@@ -219,7 +239,7 @@
         for d in range(1, nrow):
             partial_copy(s, d).start()
         for d in range(1, nrow):
-            source = lax.rem(me + d, nrow)
+            source = peer(d)
             remote(
                 part.at[s, source], part.at[s, source], p_send.at[s, d], p_recv.at[s, source],
                 (source, place),
@@ -232,9 +252,9 @@
         for c in range(CHUNKS):
             @pl.loop(0, chunk // (TILE * GROUP))
             def rotate(t):
-                held = tiles(c, t)
-                pairs = turn([(x[s, 0, rows, :], x[s, 1, rows, :]) for rows in held], turns)
-                for rows, (upper, lower) in zip(held, pairs):
+                group = tiles(c, t)
+                pairs = turn([(x[s, 0, rows, :], x[s, 1, rows, :]) for rows in group], turns)
+                for rows, (upper, lower) in zip(group, pairs):
                     r[s, 0, rows, :] = upper
                     r[s, 1, rows, :] = lower
                     x[s + 1, kept, rows, :] = upper
@@ -256,11 +276,12 @@
                 out_ref[rows, 0:B] = x[STEPS, 0, rows, :]
                 out_ref[rows, B:2 * B] = x[STEPS, 1, rows, :]
 
-    for b in range(2):
-        for d in range(nacross):
-            direct(d, b).wait_send()
-            if d:
-                forward(d, b).wait_send()
+    for q in range(PARTS):
+        for b in range(2):
+            for d in range(nacross):
+                direct(d, b, q).wait_send()
+                if d:
+                    passed_on(d, b, q, core).wait_send()
 
     @pl.loop(0, STEPS)
     def drain(s):
@@ -290,18 +311,18 @@
         out_specs=pl.BlockSpec(memory_space=pltpu.VMEM),
         scratch_shapes=[
             pltpu.SMEM((2 * npair,), jnp.int32),
-            pltpu.VMEM((2 * npair, height, B), jnp.float32),
+            *[pltpu.VMEM((2 * npair, height // PARTS, B), jnp.float32) for _ in range(PARTS)],
             pltpu.VMEM((STEPS + 1, 3, height, B), jnp.float32),
             pltpu.VMEM((STEPS, 2, height, B), jnp.float32),
             pltpu.VMEM((STEPS, nrow, BANDS, B), jnp.float32),
-            dma((nacross, 2)),
-            dma((nacross, 2)),
-            dma((2 * npair,)),
+            dma((nacross, 2, PARTS)),
+            dma((nacross, 2, PARTS)),
+            dma((2 * npair, PARTS)),
             dma((STEPS, nrow)),
             dma((STEPS, nrow)),
             dma((STEPS, 2, CHUNKS)),
             dma((STEPS, 2, CHUNKS)),
-            dma((2,)),
+            dma((2, PARTS)),
             dma,
         ],
         compiler_params=pltpu.CompilerParams(

time: 58.7 us -> 58 us (0.988)
  Pallas kernels: 56.8 us -> 56 us
    pallas_call x1, Pallas kernels: 56.8 us -> 56 us  [local(): pl.pallas_call(functools.partial(kernel, nrow, npair), out_shape=jax.Shap...]
where the time goes in v6:
time: 58 us; the launch traced here: 57.8 us
  Pallas kernels  56 us (97%)
  local copies, waits for them, and re-layouts  1.77 us (3%)
    pallas_call x1, Pallas kernels, local(): pl.pallas_call(functools.partial(kernel, nrow, npair), out_shape=jax.Shap...  56 us
    unnamed x1, local copies, waits for them, and re-layouts  1.77 us

profile of v6, /device:TPU:1, one launch (start us, length us, event | category | flops | bytes accessed | tf_op | source)
XLA Modules:
  0.0 57.8 jit_solution(14669212462730279575)
XLA Ops:
  0.0 56.0 %shard_map.28 = f32[192,512]{1,0:T(8,128)} custom-call(s32[8]{0:T(128)} %seating_ref.1, f32[192,512]{1,0:T(8,128)} %m_ref.1), custom_call_target="tpu_custom_call" | custom-call | tf_op jit(solution)/shard_map/pallas_call | solution.py:304
  56.1 1.8 %copy.4 = f32[192,512]{1,0:T(8,128)} copy(f32[192,512]{1,0:T(8,128)} %shard_map.28) | data formatting | bytes 786432

commit v7 on v6

--- a/solution.py
+++ b/solution.py
@@ -11,9 +11,9 @@
 STEPS = 4
 INNER = 4
 TILE = 8
-GROUP = 4
-CHUNKS = 6
-PARTS = 3
+GROUP = 6
+CHUNKS = 4
+PARTS = 4
 BANDS = 4 * INNER
 MESH = pl.DeviceIdType.MESH
 

time: 58 us -> 57.8 us (level)
  no operation moved by 1% of the time
where the time goes in v7:
time: 57.8 us; the launch traced here: 57.6 us
  Pallas kernels  55.8 us (97%)
  local copies, waits for them, and re-layouts  1.77 us (3%)
    pallas_call x1, Pallas kernels, local(): pl.pallas_call(functools.partial(kernel, nrow, npair), out_shape=jax.Shap...  55.8 us
    unnamed x1, local copies, waits for them, and re-layouts  1.77 us

profile of v7, /device:TPU:1, one launch (start us, length us, event | category | flops | bytes accessed | tf_op | source)
XLA Modules:
  0.0 57.6 jit_solution(8413598981038598650)
XLA Ops:
  0.0 55.8 %shard_map.28 = f32[192,512]{1,0:T(8,128)} custom-call(s32[8]{0:T(128)} %seating_ref.1, f32[192,512]{1,0:T(8,128)} %m_ref.1), custom_call_target="tpu_custom_call" | custom-call | tf_op jit(solution)/shard_map/pallas_call | solution.py:304
  55.8 1.8 %copy.4 = f32[192,512]{1,0:T(8,128)} copy(f32[192,512]{1,0:T(8,128)} %shard_map.28) | data formatting | bytes 786432
